TPU v7x, 512 devices: a whole 4x4x16 slice. The times are simulated.
512 devices in a mesh: dp: 16 (over z_hi, y), section: 8 (over x, core), tensor: 4 (over z_lo).
Axes of the slice: x: 4, y: 4, z: 16 (z_hi: 4, z_lo: 4; z = z_hi * 4 + z_lo), core: 2. Of those that a mesh axis runs over, the one named last changes fastest.
Arguments:
- x_in: bfloat16 [64, 128, 1536], P('dp', None, 'tensor'), may hold values from -6 to 6
- tangent_in: bfloat16 [64, 128, 1536], P('dp', None, 'tensor'), may hold values from -6 to 6
- timesteps: int32 [64], P('dp'), may hold values from 0 to 63
- mod_table: bfloat16 [8, 64, 6, 1536], P('section'), may hold values from -3 to 3
- w_qkv: bfloat16 [8, 1536, 3, 1536], P('section', 'dp', None, 'tensor'), may hold values from -3 to 3
- w_out: bfloat16 [8, 1536, 1536], P('section', 'dp', 'tensor'), may hold values from -0.15625 to 0.15625
Outputs:
- section_primal: bfloat16 [8, 64, 128, 1536], P('section', 'dp', None, 'tensor')
- section_tangent: bfloat16 [8, 64, 128, 1536], P('section', 'dp', None, 'tensor')
All inputs are finite; a program needn't handle non-finite values.
Results may differ from a plain program's by a relative error of at most 0.02.
Values may be sent and summed in bfloat16 or wider, within the bound.
No kernel may reach another device: no remote copies, remote signals or barrier semaphores. Data moves between devices by JAX's collectives and lax.ppermute only.
A program may use at most 64 MiB of HBM per device.

v0:
```python
import jax
import jax.numpy as jnp
from jax import lax
from jax.sharding import PartitionSpec as P

HD = 128


EPSILON = 1e-06


def from_behind(block, axis, distance):
    devices = range(lax.axis_size(axis))
    route = [(i - distance, i) for i in devices if i - distance in devices]
    return lax.ppermute(block, axis, route)


def attend(projected, d_projected, length, heads_here):
    factor = HD ** (-0.5)
    parts = projected.astype(jnp.bfloat16).reshape(length, 3, heads_here, HD)
    d_parts = d_projected.astype(jnp.bfloat16).reshape(length, 3, heads_here, HD)
    query, key_v, value = (parts[:, 0], parts[:, 1], parts[:, 2])
    d_query, d_key, d_value = (d_parts[:, 0], d_parts[:, 1], d_parts[:, 2])
    scores = jnp.einsum("lhe,mhe->hlm", query, key_v, preferred_element_type=jnp.float32) * factor
    soft_w = jax.nn.softmax(scores, axis=-1)
    d_scores = (
        jnp.einsum("lhe,mhe->hlm", d_query, key_v, preferred_element_type=jnp.float32)
        + jnp.einsum("lhe,mhe->hlm", query, d_key, preferred_element_type=jnp.float32)
    ) * factor
    d_soft = soft_w * (d_scores - jnp.sum(soft_w * d_scores, -1, keepdims=True))
    soft_b = soft_w.astype(jnp.bfloat16)
    d_soft_b = d_soft.astype(jnp.bfloat16)
    head_out = jnp.einsum("hlm,mhe->lhe", soft_b, value, preferred_element_type=jnp.float32)
    d_head = jnp.einsum(
        "hlm,mhe->lhe", d_soft_b, value, preferred_element_type=jnp.float32
    ) + jnp.einsum("hlm,mhe->lhe", soft_b, d_value, preferred_element_type=jnp.float32)
    return (
        head_out.astype(jnp.bfloat16).reshape(length, -1),
        d_head.astype(jnp.bfloat16).reshape(length, -1),
    )


def body(x_in, tangent_in, timesteps, mod_table, w_qkv, w_out):
    micro_count, length, width_part = x_in.shape
    tensor_count = lax.axis_size("tensor")
    section_count = lax.axis_size("section")
    section_pos = lax.axis_index("section")
    tensor_pos = lax.axis_index("tensor")
    full_width = width_part * tensor_count
    levels = mod_table.shape[1]
    full_qkv, full_out = (
        lax.all_gather(w_qkv, "dp", axis=1, tiled=True),
        lax.all_gather(w_out, "dp", axis=1, tiled=True),
    )
    w_in = full_qkv[0].reshape(full_width, -1)
    w_proj = full_out[0]
    columns = w_in.shape[1]
    local_cols = columns // 3
    heads_here = local_cols // HD
    onehot = (timesteps[:, None] == jnp.arange(levels, dtype=jnp.int32)[None, :]).astype(
        jnp.bfloat16
    )
    modulation = jnp.dot(
        onehot, mod_table[0].reshape(levels, 6 * full_width), preferred_element_type=jnp.float32
    )
    modulation = modulation.reshape(micro_count, 6, full_width)
    own_mods = lax.dynamic_slice_in_dim(modulation, tensor_pos * width_part, width_part, 2)

    def section_layer(which_micro, active, primal, tangent):
        mod_row = lax.dynamic_index_in_dim(modulation, which_micro, 0, keepdims=False)
        own_row = lax.dynamic_index_in_dim(own_mods, which_micro, 0, keepdims=False)
        x_float = primal.astype(jnp.float32)
        v_float = tangent.astype(jnp.float32)
        empty_in = jnp.zeros((length, columns), jnp.float32)
        rows_x, rows_v = (
            lax.all_gather(primal, "tensor", axis=1, tiled=True),
            lax.all_gather(tangent, "tensor", axis=1, tiled=True),
        )
        all_x = rows_x.astype(jnp.float32)
        all_v = rows_v.astype(jnp.float32)
        row_mean = jnp.mean(all_x, -1, keepdims=True)
        centred = all_x - row_mean
        inv_std = lax.rsqrt(jnp.mean(centred * centred, -1, keepdims=True) + EPSILON)
        normed = centred * inv_std
        tan_centred = all_v - jnp.mean(all_v, -1, keepdims=True)
        dnormed = inv_std * (
            tan_centred - normed * jnp.mean(normed * tan_centred, -1, keepdims=True)
        )
        hidden_in = (normed * (1.0 + mod_row[1]) + mod_row[0]).astype(jnp.bfloat16)
        d_hidden = (dnormed * (1.0 + mod_row[1]) + normed * mod_row[4] + mod_row[3]).astype(
            jnp.bfloat16
        )
        projected, d_projected = lax.cond(
            active,
            lambda: (
                jnp.dot(hidden_in, w_in, preferred_element_type=jnp.float32),
                jnp.dot(d_hidden, w_in, preferred_element_type=jnp.float32),
            ),
            lambda: (empty_in, empty_in),
        )
        empty_heads = jnp.zeros((length, local_cols), jnp.bfloat16)
        head_out, d_head = lax.cond(
            active,
            lambda: attend(projected, d_projected, length, heads_here),
            lambda: (empty_heads, empty_heads),
        )
        empty_out = jnp.zeros((length, width_part), jnp.float32)
        totals = (empty_out, empty_out)
        pieces = (
            lax.all_gather(head_out, "tensor", axis=1, tiled=True),
            lax.all_gather(d_head, "tensor", axis=1, tiled=True),
        )
        attn_out, d_attn = lax.cond(
            active,
            lambda: (
                jnp.dot(pieces[0], w_proj, preferred_element_type=jnp.float32),
                jnp.dot(pieces[1], w_proj, preferred_element_type=jnp.float32),
            ),
            lambda: totals,
        )
        new_primal = (x_float + own_row[2] * attn_out).astype(jnp.bfloat16)
        new_tangent = (v_float + own_row[2] * d_attn + own_row[5] * attn_out).astype(jnp.bfloat16)
        return (new_primal, new_tangent)

    def run_tick(tick_num, carry):
        recv_x, recv_v, keep_x, keep_v = carry
        which_micro = tick_num - section_pos
        active = jnp.logical_and(which_micro >= 0, which_micro < micro_count)
        clipped = jnp.clip(which_micro, 0, micro_count - 1)
        first_section = section_pos == 0
        primal = jnp.where(
            first_section, lax.dynamic_index_in_dim(x_in, clipped, 0, keepdims=False), recv_x
        )
        tangent = jnp.where(
            first_section, lax.dynamic_index_in_dim(tangent_in, clipped, 0, keepdims=False), recv_v
        )
        new_primal, new_tangent = section_layer(clipped, active, primal, tangent)
        old_x = lax.dynamic_index_in_dim(keep_x, clipped, 0, keepdims=False)
        old_v = lax.dynamic_index_in_dim(keep_v, clipped, 0, keepdims=False)
        keep_x = lax.dynamic_update_index_in_dim(
            keep_x, jnp.where(active, new_primal, old_x), clipped, 0
        )
        keep_v = lax.dynamic_update_index_in_dim(
            keep_v, jnp.where(active, new_tangent, old_v), clipped, 0
        )
        return (new_primal, new_tangent, keep_x, keep_v)

    def advance(tick_num, carry):
        new_primal, new_tangent, keep_x, keep_v = run_tick(tick_num, carry)
        sent_x, sent_v = from_behind((new_primal, new_tangent), "section", 1)
        return (sent_x, sent_v, keep_x, keep_v)

    total_ticks = micro_count + section_count - 1
    empty_act = jnp.zeros((length, width_part), jnp.bfloat16)
    start_state = (empty_act, empty_act, jnp.zeros_like(x_in), jnp.zeros_like(tangent_in))
    state = lax.fori_loop(0, total_ticks - 1, advance, start_state)
    final_state = run_tick(total_ticks - 1, state)
    return (final_state[2][None], final_state[3][None])


def solution(mesh):
    in_specs = (
        P("dp", None, "tensor"),
        P("dp", None, "tensor"),
        P("dp"),
        P("section", None, None, None),
        P("section", "dp", None, "tensor"),
        P("section", "dp", "tensor"),
    )
    out_specs = (P("section", "dp", None, "tensor"), P("section", "dp", None, "tensor"))
    return jax.shard_map(body, mesh=mesh, in_specs=in_specs, out_specs=out_specs, check_vma=False)
```

profile of v0, /device:TPU:7, one launch (start us, length us, event | category | flops | bytes accessed | tf_op | source)
XLA Modules:
  0.0 1047.7 jit_solution(16794523792232117872)
XLA Ops:
  11.7 122.8 %all-gather.3.cloned.1.call-done = bf16[1,1536,3,384]{3,1,2,0:T(8,128)(2,1)} async-done(((bf16[1,96,3,384]{3,1,2,0:T(8,128)(2,1)}), bf16[1,1536,3,384]{3,1,2,0:T(8,128)(2,1)}) %all-gather.3.cloned.1.call-update) | async-done | bytes 3538960 | tf_op jit(solution)/shard_map/all_gather | solution.py:52
  146.4 68.5 %all-gather.5.cloned.1.call-done = bf16[1,1536,384]{2,1,0:T(8,128)(2,1)} async-done(((bf16[1,96,384]{2,1,0:T(8,128)(2,1)}), bf16[1,1536,384]{2,1,0:T(8,128)(2,1)}) %all-gather.5.cloned.1.call-update) | async-done | bytes 1179664 | tf_op jit(solution)/shard_map/all_gather | solution.py:53
  216.5 762.0 %while.20 = (s32[]{:T(128)}, bf16[128,384]{1,0:T(8,128)(2,1)S(1)}, bf16[128,384]{1,0:T(8,128)(2,1)S(1)}, bf16[4,128,384]{2,1,0:T(8,128)(2,1)}, bf16[4,128,384]{2...) while((s32[]{:T(128)}, bf16[128,384]{1,0:T(8,128)(2,1)S(1)}, ...), condition=%wide.region_14.15_spmd, body=%wide.region_0.14_spmd.sunk | while | flops 1329220480 | bytes 45423756 | solution.py:156
  230.3 12.9 %all_gather.60 = bf16[128,1536]{1,0:T(8,128)(2,1)S(1)} all-gather(bf16[128,384]{1,0:T(8,128)(2,1)S(1)} %bitcast_select_fusion.8), channel_id=1, replica_groups=mesh['dp'=16,'section'=8,'tensor'=4] {'tensor'}, dimensions={1}, use_global_device_ids=true | all-gather | bytes 491520 | tf_op jit(solution)/shard_map/while/body/eval_jaxpr/all_gather | solution.py:77
  273.6 12.5 %collective-permute-done = bf16[128,384]{1,0:T(8,128)(2,1)S(1)} collective-permute-done((bf16[128,384]{1,0:T(8,128)(2,1)S(1)}, bf16[128,384]{1,0:T(8,128)(2,1)S(1)}, u32[]{:S(2)}, u32[]{:S(2)}) %collective-permute-start) | collective-permute-done | bytes 98336 | tf_op jit(solution)/shard_map/while/body/eval_jaxpr/ppermute | solution.py:15
  289.0 12.6 %all_gather.61 = bf16[128,1536]{1,0:T(8,128)(2,1)S(1)} all-gather(bf16[128,384]{1,0:T(8,128)(2,1)S(1)} %bitcast_select_fusion.9), channel_id=1, replica_groups=mesh['dp'=16,'section'=8,'tensor'=4] {'tensor'}, dimensions={1}, use_global_device_ids=true | all-gather | bytes 491520 | tf_op jit(solution)/shard_map/while/body/eval_jaxpr/all_gather | solution.py:76
  329.1 12.9 %all_gather.63 = bf16[128,1536]{1,0:T(8,128)(2,1)S(1)} all-gather(bf16[128,384]{1,0:T(8,128)(2,1)S(1)} %copy.121), channel_id=1, replica_groups=mesh['dp'=16,'section'=8,'tensor'=4] {'tensor'}, dimensions={1}, use_global_device_ids=true | all-gather | bytes 491520 | tf_op jit(solution)/shard_map/while/body/eval_jaxpr/all_gather | solution.py:111
  388.1 12.7 %all_gather.62 = bf16[128,1536]{1,0:T(8,128)(2,1)S(1)} all-gather(bf16[128,384]{1,0:T(8,128)(2,1)S(1)} %copy.120), channel_id=1, replica_groups=mesh['dp'=16,'section'=8,'tensor'=4] {'tensor'}, dimensions={1}, use_global_device_ids=true | all-gather | bytes 491520 | tf_op jit(solution)/shard_map/while/body/eval_jaxpr/all_gather | solution.py:110
  401.0 12.8 %all_gather.63 = bf16[128,1536]{1,0:T(8,128)(2,1)S(1)} all-gather(bf16[128,384]{1,0:T(8,128)(2,1)S(1)} %copy.121), channel_id=1, replica_groups=mesh['dp'=16,'section'=8,'tensor'=4] {'tensor'}, dimensions={1}, use_global_device_ids=true | all-gather | bytes 491520 | tf_op jit(solution)/shard_map/while/body/eval_jaxpr/all_gather | solution.py:111
  418.9 14.0 %collective-permute-done = bf16[128,384]{1,0:T(8,128)(2,1)S(1)} collective-permute-done((bf16[128,384]{1,0:T(8,128)(2,1)S(1)}, bf16[128,384]{1,0:T(8,128)(2,1)S(1)}, u32[]{:S(2)}, u32[]{:S(2)}) %collective-permute-start) | collective-permute-done | bytes 98336 | tf_op jit(solution)/shard_map/while/body/eval_jaxpr/ppermute | solution.py:15
  462.6 12.8 %all_gather.62 = bf16[128,1536]{1,0:T(8,128)(2,1)S(1)} all-gather(bf16[128,384]{1,0:T(8,128)(2,1)S(1)} %copy.120), channel_id=1, replica_groups=mesh['dp'=16,'section'=8,'tensor'=4] {'tensor'}, dimensions={1}, use_global_device_ids=true | all-gather | bytes 491520 | tf_op jit(solution)/shard_map/while/body/eval_jaxpr/all_gather | solution.py:110
  475.5 13.1 %all_gather.63 = bf16[128,1536]{1,0:T(8,128)(2,1)S(1)} all-gather(bf16[128,384]{1,0:T(8,128)(2,1)S(1)} %copy.121), channel_id=1, replica_groups=mesh['dp'=16,'section'=8,'tensor'=4] {'tensor'}, dimensions={1}, use_global_device_ids=true | all-gather | bytes 491520 | tf_op jit(solution)/shard_map/while/body/eval_jaxpr/all_gather | solution.py:111
  547.0 12.9 %all_gather.63 = bf16[128,1536]{1,0:T(8,128)(2,1)S(1)} all-gather(bf16[128,384]{1,0:T(8,128)(2,1)S(1)} %copy.121), channel_id=1, replica_groups=mesh['dp'=16,'section'=8,'tensor'=4] {'tensor'}, dimensions={1}, use_global_device_ids=true | all-gather | bytes 491520 | tf_op jit(solution)/shard_map/while/body/eval_jaxpr/all_gather | solution.py:111
  565.1 14.1 %collective-permute-done = bf16[128,384]{1,0:T(8,128)(2,1)S(1)} collective-permute-done((bf16[128,384]{1,0:T(8,128)(2,1)S(1)}, bf16[128,384]{1,0:T(8,128)(2,1)S(1)}, u32[]{:S(2)}, u32[]{:S(2)}) %collective-permute-start) | collective-permute-done | bytes 98336 | tf_op jit(solution)/shard_map/while/body/eval_jaxpr/ppermute | solution.py:15
  608.5 13.2 %all_gather.62 = bf16[128,1536]{1,0:T(8,128)(2,1)S(1)} all-gather(bf16[128,384]{1,0:T(8,128)(2,1)S(1)} %copy.120), channel_id=1, replica_groups=mesh['dp'=16,'section'=8,'tensor'=4] {'tensor'}, dimensions={1}, use_global_device_ids=true | all-gather | bytes 491520 | tf_op jit(solution)/shard_map/while/body/eval_jaxpr/all_gather | solution.py:110
  621.9 12.4 %all_gather.63 = bf16[128,1536]{1,0:T(8,128)(2,1)S(1)} all-gather(bf16[128,384]{1,0:T(8,128)(2,1)S(1)} %copy.121), channel_id=1, replica_groups=mesh['dp'=16,'section'=8,'tensor'=4] {'tensor'}, dimensions={1}, use_global_device_ids=true | all-gather | bytes 491520 | tf_op jit(solution)/shard_map/while/body/eval_jaxpr/all_gather | solution.py:111
  639.5 14.0 %collective-permute-done = bf16[128,384]{1,0:T(8,128)(2,1)S(1)} collective-permute-done((bf16[128,384]{1,0:T(8,128)(2,1)S(1)}, bf16[128,384]{1,0:T(8,128)(2,1)S(1)}, u32[]{:S(2)}, u32[]{:S(2)}) %collective-permute-start) | collective-permute-done | bytes 98336 | tf_op jit(solution)/shard_map/while/body/eval_jaxpr/ppermute | solution.py:15
  656.3 12.4 %all_gather.61 = bf16[128,1536]{1,0:T(8,128)(2,1)S(1)} all-gather(bf16[128,384]{1,0:T(8,128)(2,1)S(1)} %bitcast_select_fusion.9), channel_id=1, replica_groups=mesh['dp'=16,'section'=8,'tensor'=4] {'tensor'}, dimensions={1}, use_global_device_ids=true | all-gather | bytes 491520 | tf_op jit(solution)/shard_map/while/body/eval_jaxpr/all_gather | solution.py:76
  713.2 23.6 %collective-permute-done = bf16[128,384]{1,0:T(8,128)(2,1)S(1)} collective-permute-done((bf16[128,384]{1,0:T(8,128)(2,1)S(1)}, bf16[128,384]{1,0:T(8,128)(2,1)S(1)}, u32[]{:S(2)}, u32[]{:S(2)}) %collective-permute-start) | collective-permute-done | bytes 98336 | tf_op jit(solution)/shard_map/while/body/eval_jaxpr/ppermute | solution.py:15
  739.7 13.1 %all_gather.61 = bf16[128,1536]{1,0:T(8,128)(2,1)S(1)} all-gather(bf16[128,384]{1,0:T(8,128)(2,1)S(1)} %bitcast_select_fusion.9), channel_id=1, replica_groups=mesh['dp'=16,'section'=8,'tensor'=4] {'tensor'}, dimensions={1}, use_global_device_ids=true | all-gather | bytes 491520 | tf_op jit(solution)/shard_map/while/body/eval_jaxpr/all_gather | solution.py:76
  785.4 13.1 %all_gather.63 = bf16[128,1536]{1,0:T(8,128)(2,1)S(1)} all-gather(bf16[128,384]{1,0:T(8,128)(2,1)S(1)} %copy.121), channel_id=1, replica_groups=mesh['dp'=16,'section'=8,'tensor'=4] {'tensor'}, dimensions={1}, use_global_device_ids=true | all-gather | bytes 491520 | tf_op jit(solution)/shard_map/while/body/eval_jaxpr/all_gather | solution.py:111
  863.9 12.9 %all_gather.63 = bf16[128,1536]{1,0:T(8,128)(2,1)S(1)} all-gather(bf16[128,384]{1,0:T(8,128)(2,1)S(1)} %copy.121), channel_id=1, replica_groups=mesh['dp'=16,'section'=8,'tensor'=4] {'tensor'}, dimensions={1}, use_global_device_ids=true | all-gather | bytes 491520 | tf_op jit(solution)/shard_map/while/body/eval_jaxpr/all_gather | solution.py:111
  882.7 14.0 %collective-permute-done = bf16[128,384]{1,0:T(8,128)(2,1)S(1)} collective-permute-done((bf16[128,384]{1,0:T(8,128)(2,1)S(1)}, bf16[128,384]{1,0:T(8,128)(2,1)S(1)}, u32[]{:S(2)}, u32[]{:S(2)}) %collective-permute-start) | collective-permute-done | bytes 98336 | tf_op jit(solution)/shard_map/while/body/eval_jaxpr/ppermute | solution.py:15
  961.8 14.7 %collective-permute-done = bf16[128,384]{1,0:T(8,128)(2,1)S(1)} collective-permute-done((bf16[128,384]{1,0:T(8,128)(2,1)S(1)}, bf16[128,384]{1,0:T(8,128)(2,1)S(1)}, u32[]{:S(2)}, u32[]{:S(2)}) %collective-permute-start) | collective-permute-done | bytes 98336 | tf_op jit(solution)/shard_map/while/body/eval_jaxpr/ppermute | solution.py:15
  (476 shorter events, 581.5 us)
Async XLA Ops:
  7.2 127.3 %all-gather.3.cloned.1.call-start = ((), (), s32[]{:S(2)}) async-start(), calls=%async_computation | async-start | bytes 3760128 | tf_op jit(solution)/shard_map/all_gather | solution.py:52
  7.9 206.9 %all-gather.5.cloned.1.call-start = ((), (), s32[]{:S(2)}) async-start(), calls=%async_computation.1 | async-start | bytes 1253376 | tf_op jit(solution)/shard_map/all_gather | solution.py:53
  271.0 15.1 %collective-permute-start = (bf16[128,384]{1,0:T(8,128)(2,1)S(1)}, bf16[128,384]{1,0:T(8,128)(2,1)S(1)}, u32[]{:S(2)}, u32[]{:S(2)}) collective-permute-start(bf16[128,384]{1,0:T(8,128)(2,1)S(1)} %get-tuple-element.545), channel_id=1, source_target_pairs={{0,4},{4,8},{8,12},{12,16},{16,20},{20,24},{24,28},{1,5},{5,9},{9,... | collective-permute-start | bytes 294920 | tf_op jit(solution)/shard_map/while/body/eval_jaxpr/ppermute | solution.py:15
  272.2 15.8 %collective-permute-start.1 = (bf16[128,384]{1,0:T(8,128)(2,1)S(1)}, bf16[128,384]{1,0:T(8,128)(2,1)S(1)}, u32[]{:S(2)}, u32[]{:S(2)}) collective-permute-start(bf16[128,384]{1,0:T(8,128)(2,1)S(1)} %get-tuple-element.546), channel_id=1, source_target_pairs={{0,4},{4,8},{8,12},{12,16},{16,20},{20,24},{24,28},{1,5},{5,9},{9,... | collective-permute-start | bytes 294920 | tf_op jit(solution)/shard_map/while/body/eval_jaxpr/ppermute | solution.py:15
  344.6 14.6 %collective-permute-start = (bf16[128,384]{1,0:T(8,128)(2,1)S(1)}, bf16[128,384]{1,0:T(8,128)(2,1)S(1)}, u32[]{:S(2)}, u32[]{:S(2)}) collective-permute-start(bf16[128,384]{1,0:T(8,128)(2,1)S(1)} %get-tuple-element.545), channel_id=1, source_target_pairs={{0,4},{4,8},{8,12},{12,16},{16,20},{20,24},{24,28},{1,5},{5,9},{9,... | collective-permute-start | bytes 294920 | tf_op jit(solution)/shard_map/while/body/eval_jaxpr/ppermute | solution.py:15
  345.9 15.2 %collective-permute-start.1 = (bf16[128,384]{1,0:T(8,128)(2,1)S(1)}, bf16[128,384]{1,0:T(8,128)(2,1)S(1)}, u32[]{:S(2)}, u32[]{:S(2)}) collective-permute-start(bf16[128,384]{1,0:T(8,128)(2,1)S(1)} %get-tuple-element.546), channel_id=1, source_target_pairs={{0,4},{4,8},{8,12},{12,16},{16,20},{20,24},{24,28},{1,5},{5,9},{9,... | collective-permute-start | bytes 294920 | tf_op jit(solution)/shard_map/while/body/eval_jaxpr/ppermute | solution.py:15
  416.4 16.6 %collective-permute-start = (bf16[128,384]{1,0:T(8,128)(2,1)S(1)}, bf16[128,384]{1,0:T(8,128)(2,1)S(1)}, u32[]{:S(2)}, u32[]{:S(2)}) collective-permute-start(bf16[128,384]{1,0:T(8,128)(2,1)S(1)} %get-tuple-element.545), channel_id=1, source_target_pairs={{0,4},{4,8},{8,12},{12,16},{16,20},{20,24},{24,28},{1,5},{5,9},{9,... | collective-permute-start | bytes 294920 | tf_op jit(solution)/shard_map/while/body/eval_jaxpr/ppermute | solution.py:15
  417.6 17.2 %collective-permute-start.1 = (bf16[128,384]{1,0:T(8,128)(2,1)S(1)}, bf16[128,384]{1,0:T(8,128)(2,1)S(1)}, u32[]{:S(2)}, u32[]{:S(2)}) collective-permute-start(bf16[128,384]{1,0:T(8,128)(2,1)S(1)} %get-tuple-element.546), channel_id=1, source_target_pairs={{0,4},{4,8},{8,12},{12,16},{16,20},{20,24},{24,28},{1,5},{5,9},{9,... | collective-permute-start | bytes 294920 | tf_op jit(solution)/shard_map/while/body/eval_jaxpr/ppermute | solution.py:15
  491.2 14.9 %collective-permute-start = (bf16[128,384]{1,0:T(8,128)(2,1)S(1)}, bf16[128,384]{1,0:T(8,128)(2,1)S(1)}, u32[]{:S(2)}, u32[]{:S(2)}) collective-permute-start(bf16[128,384]{1,0:T(8,128)(2,1)S(1)} %get-tuple-element.545), channel_id=1, source_target_pairs={{0,4},{4,8},{8,12},{12,16},{16,20},{20,24},{24,28},{1,5},{5,9},{9,... | collective-permute-start | bytes 294920 | tf_op jit(solution)/shard_map/while/body/eval_jaxpr/ppermute | solution.py:15
  492.5 15.6 %collective-permute-start.1 = (bf16[128,384]{1,0:T(8,128)(2,1)S(1)}, bf16[128,384]{1,0:T(8,128)(2,1)S(1)}, u32[]{:S(2)}, u32[]{:S(2)}) collective-permute-start(bf16[128,384]{1,0:T(8,128)(2,1)S(1)} %get-tuple-element.546), channel_id=1, source_target_pairs={{0,4},{4,8},{8,12},{12,16},{16,20},{20,24},{24,28},{1,5},{5,9},{9,... | collective-permute-start | bytes 294920 | tf_op jit(solution)/shard_map/while/body/eval_jaxpr/ppermute | solution.py:15
  562.5 16.7 %collective-permute-start = (bf16[128,384]{1,0:T(8,128)(2,1)S(1)}, bf16[128,384]{1,0:T(8,128)(2,1)S(1)}, u32[]{:S(2)}, u32[]{:S(2)}) collective-permute-start(bf16[128,384]{1,0:T(8,128)(2,1)S(1)} %get-tuple-element.545), channel_id=1, source_target_pairs={{0,4},{4,8},{8,12},{12,16},{16,20},{20,24},{24,28},{1,5},{5,9},{9,... | collective-permute-start | bytes 294920 | tf_op jit(solution)/shard_map/while/body/eval_jaxpr/ppermute | solution.py:15
  563.8 17.3 %collective-permute-start.1 = (bf16[128,384]{1,0:T(8,128)(2,1)S(1)}, bf16[128,384]{1,0:T(8,128)(2,1)S(1)}, u32[]{:S(2)}, u32[]{:S(2)}) collective-permute-start(bf16[128,384]{1,0:T(8,128)(2,1)S(1)} %get-tuple-element.546), channel_id=1, source_target_pairs={{0,4},{4,8},{8,12},{12,16},{16,20},{20,24},{24,28},{1,5},{5,9},{9,... | collective-permute-start | bytes 294920 | tf_op jit(solution)/shard_map/while/body/eval_jaxpr/ppermute | solution.py:15
  636.9 16.6 %collective-permute-start = (bf16[128,384]{1,0:T(8,128)(2,1)S(1)}, bf16[128,384]{1,0:T(8,128)(2,1)S(1)}, u32[]{:S(2)}, u32[]{:S(2)}) collective-permute-start(bf16[128,384]{1,0:T(8,128)(2,1)S(1)} %get-tuple-element.545), channel_id=1, source_target_pairs={{0,4},{4,8},{8,12},{12,16},{16,20},{20,24},{24,28},{1,5},{5,9},{9,... | collective-permute-start | bytes 294920 | tf_op jit(solution)/shard_map/while/body/eval_jaxpr/ppermute | solution.py:15
  638.2 17.2 %collective-permute-start.1 = (bf16[128,384]{1,0:T(8,128)(2,1)S(1)}, bf16[128,384]{1,0:T(8,128)(2,1)S(1)}, u32[]{:S(2)}, u32[]{:S(2)}) collective-permute-start(bf16[128,384]{1,0:T(8,128)(2,1)S(1)} %get-tuple-element.546), channel_id=1, source_target_pairs={{0,4},{4,8},{8,12},{12,16},{16,20},{20,24},{24,28},{1,5},{5,9},{9,... | collective-permute-start | bytes 294920 | tf_op jit(solution)/shard_map/while/body/eval_jaxpr/ppermute | solution.py:15
  708.1 30.7 %copy-start.11 = (f32[4,6,1536]{2,0,1:T(4,128)S(1)}, f32[4,6,1536]{2,0,1:T(4,128)}, u32[]{:S(2)}) copy-start(f32[4,6,1536]{2,0,1:T(4,128)} %copy-done.10) | copy-start | bytes 442372 | tf_op jit(solution)/shard_map/while
  710.6 26.2 %collective-permute-start = (bf16[128,384]{1,0:T(8,128)(2,1)S(1)}, bf16[128,384]{1,0:T(8,128)(2,1)S(1)}, u32[]{:S(2)}, u32[]{:S(2)}) collective-permute-start(bf16[128,384]{1,0:T(8,128)(2,1)S(1)} %get-tuple-element.545), channel_id=1, source_target_pairs={{0,4},{4,8},{8,12},{12,16},{16,20},{20,24},{24,28},{1,5},{5,9},{9,... | collective-permute-start | bytes 294920 | tf_op jit(solution)/shard_map/while/body/eval_jaxpr/ppermute | solution.py:15
  711.9 26.8 %collective-permute-start.1 = (bf16[128,384]{1,0:T(8,128)(2,1)S(1)}, bf16[128,384]{1,0:T(8,128)(2,1)S(1)}, u32[]{:S(2)}, u32[]{:S(2)}) collective-permute-start(bf16[128,384]{1,0:T(8,128)(2,1)S(1)} %get-tuple-element.546), channel_id=1, source_target_pairs={{0,4},{4,8},{8,12},{12,16},{16,20},{20,24},{24,28},{1,5},{5,9},{9,... | collective-permute-start | bytes 294920 | tf_op jit(solution)/shard_map/while/body/eval_jaxpr/ppermute | solution.py:15
  738.7 27.8 %copy-start.10 = (f32[4,6,1536]{2,0,1:T(4,128)}, f32[4,6,1536]{2,0,1:T(4,128)S(1)}, u32[]{:S(2)}) copy-start(f32[4,6,1536]{2,0,1:T(4,128)S(1)} %get-tuple-element.614) | copy-start | bytes 442372 | tf_op jit(solution)/shard_map/while
  801.8 14.3 %collective-permute-start = (bf16[128,384]{1,0:T(8,128)(2,1)S(1)}, bf16[128,384]{1,0:T(8,128)(2,1)S(1)}, u32[]{:S(2)}, u32[]{:S(2)}) collective-permute-start(bf16[128,384]{1,0:T(8,128)(2,1)S(1)} %get-tuple-element.545), channel_id=1, source_target_pairs={{0,4},{4,8},{8,12},{12,16},{16,20},{20,24},{24,28},{1,5},{5,9},{9,... | collective-permute-start | bytes 294920 | tf_op jit(solution)/shard_map/while/body/eval_jaxpr/ppermute | solution.py:15
  803.1 15.0 %collective-permute-start.1 = (bf16[128,384]{1,0:T(8,128)(2,1)S(1)}, bf16[128,384]{1,0:T(8,128)(2,1)S(1)}, u32[]{:S(2)}, u32[]{:S(2)}) collective-permute-start(bf16[128,384]{1,0:T(8,128)(2,1)S(1)} %get-tuple-element.546), channel_id=1, source_target_pairs={{0,4},{4,8},{8,12},{12,16},{16,20},{20,24},{24,28},{1,5},{5,9},{9,... | collective-permute-start | bytes 294920 | tf_op jit(solution)/shard_map/while/body/eval_jaxpr/ppermute | solution.py:15
  880.1 16.6 %collective-permute-start = (bf16[128,384]{1,0:T(8,128)(2,1)S(1)}, bf16[128,384]{1,0:T(8,128)(2,1)S(1)}, u32[]{:S(2)}, u32[]{:S(2)}) collective-permute-start(bf16[128,384]{1,0:T(8,128)(2,1)S(1)} %get-tuple-element.545), channel_id=1, source_target_pairs={{0,4},{4,8},{8,12},{12,16},{16,20},{20,24},{24,28},{1,5},{5,9},{9,... | collective-permute-start | bytes 294920 | tf_op jit(solution)/shard_map/while/body/eval_jaxpr/ppermute | solution.py:15
  881.4 17.2 %collective-permute-start.1 = (bf16[128,384]{1,0:T(8,128)(2,1)S(1)}, bf16[128,384]{1,0:T(8,128)(2,1)S(1)}, u32[]{:S(2)}, u32[]{:S(2)}) collective-permute-start(bf16[128,384]{1,0:T(8,128)(2,1)S(1)} %get-tuple-element.546), channel_id=1, source_target_pairs={{0,4},{4,8},{8,12},{12,16},{16,20},{20,24},{24,28},{1,5},{5,9},{9,... | collective-permute-start | bytes 294920 | tf_op jit(solution)/shard_map/while/body/eval_jaxpr/ppermute | solution.py:15
  959.3 17.3 %collective-permute-start = (bf16[128,384]{1,0:T(8,128)(2,1)S(1)}, bf16[128,384]{1,0:T(8,128)(2,1)S(1)}, u32[]{:S(2)}, u32[]{:S(2)}) collective-permute-start(bf16[128,384]{1,0:T(8,128)(2,1)S(1)} %get-tuple-element.545), channel_id=1, source_target_pairs={{0,4},{4,8},{8,12},{12,16},{16,20},{20,24},{24,28},{1,5},{5,9},{9,... | collective-permute-start | bytes 294920 | tf_op jit(solution)/shard_map/while/body/eval_jaxpr/ppermute | solution.py:15
  960.5 17.9 %collective-permute-start.1 = (bf16[128,384]{1,0:T(8,128)(2,1)S(1)}, bf16[128,384]{1,0:T(8,128)(2,1)S(1)}, u32[]{:S(2)}, u32[]{:S(2)}) collective-permute-start(bf16[128,384]{1,0:T(8,128)(2,1)S(1)} %get-tuple-element.546), channel_id=1, source_target_pairs={{0,4},{4,8},{8,12},{12,16},{16,20},{20,24},{24,28},{1,5},{5,9},{9,... | collective-permute-start | bytes 294920 | tf_op jit(solution)/shard_map/while/body/eval_jaxpr/ppermute | solution.py:15
  (43 other events, 835.7 us)
Sparse Core Ops, SparseCore 0:
  11.0 123.4 all-gather.2
  137.5 77.3 all-gather.4
where the time goes:
time: 1060 us; the launch traced here: 1050 us
  blocking collectives  536 us (51%)
  waiting for transfers between devices  355 us (33%)
  other arithmetic  47.4 us (4%)
  local copies, waits for them, and re-layouts  41.7 us (4%)
  starting transfers between devices  25.8 us (2%)
  matrix products  25.2 us (2%)
  between operations  14.3 us (1%)
    ppermute x20, waiting for transfers between devices, from_behind(): return lax.ppermute(block, axis, route)  162 us
    all_gather x11, blocking collectives, section_layer(): lax.all_gather(d_head, 'tensor', axis=1, tiled=True)  138 us
    all_gather x11, blocking collectives, section_layer(): lax.all_gather(head_out, 'tensor', axis=1, tiled=True)  134 us
    all_gather x11, blocking collectives, section_layer(): lax.all_gather(tangent, 'tensor', axis=1, tiled=True)  133 us
    all_gather x11, blocking collectives, section_layer(): lax.all_gather(primal, 'tensor', axis=1, tiled=True)  132 us
    all_gather x1, waiting for transfers between devices, body(): lax.all_gather(w_qkv, 'dp', axis=1, tiled=True)  123 us
    all_gather x1, waiting for transfers between devices, body(): lax.all_gather(w_out, 'dp', axis=1, tiled=True)  68.5 us
    ppermute x20, starting transfers between devices, from_behind(): return lax.ppermute(block, axis, route)  25.7 us
  transfers between devices with their start and end apart: 22, of which 22 were waited for; matrix products, arithmetic and copies ran while one was open for 1% of the time, Pallas kernels for 0%

commit v1 on v0

v1 whole, which is shorter than its diff:
```python
import jax
import jax.numpy as jnp
import numpy as np
from jax import lax
from jax.experimental import pallas as pl
from jax.experimental.pallas import tpu as pltpu
from jax.sharding import Mesh, PartitionSpec as P

HD = 128
EPSILON = 1e-06
LONG = 64

BF = jnp.bfloat16
F32 = jnp.float32


def dot(a, b, dims=((1,), (0,))):
    return lax.dot_general(a, b, (dims, ((), ())), preferred_element_type=F32)


def layer_kernel(xv_ref, mod_ref, wl_ref, ws_ref, out_ref, w_in, w_proj, heads, sems):
    groups, z_hi, ys, rows, cols = w_in.shape
    width = xv_ref.shape[1]
    length = xv_ref.shape[0] // 2
    part = width // groups
    for g in range(groups):
        for y in range(ys):
            pltpu.make_async_copy(
                wl_ref.at[y, :, g, :, pl.ds(0, cols)], w_in.at[g, :, y, pl.ds(0, LONG)], sems.at[g]
            ).start()
        pltpu.make_async_copy(
            ws_ref.at[:, g, :, :, pl.ds(0, cols)],
            w_in.at[g, :, :, pl.ds(LONG, rows - LONG)],
            sems.at[g],
        ).start()
    for g in range(groups):
        lanes = pl.ds(g * part, part)
        for y in range(ys):
            pltpu.make_async_copy(
                wl_ref.at[y, :, g, :, pl.ds(cols, part)],
                w_proj.at[:, y, pl.ds(0, LONG), lanes],
                sems.at[groups],
            ).start()
        pltpu.make_async_copy(
            ws_ref.at[:, g, :, :, pl.ds(cols, part)],
            w_proj.at[:, :, pl.ds(LONG, rows - LONG), lanes],
            sems.at[groups],
        ).start()

    x = xv_ref[:length].astype(F32)
    v = xv_ref[length:].astype(F32)
    centred = x - jnp.mean(x, -1, keepdims=True)
    inv_std = lax.rsqrt(jnp.mean(centred * centred, -1, keepdims=True) + EPSILON)
    normed = centred * inv_std
    tan_centred = v - jnp.mean(v, -1, keepdims=True)
    dnormed = inv_std * (
        tan_centred - normed * jnp.mean(normed * tan_centred, -1, keepdims=True)
    )
    gain = 1.0 + mod_ref[1:2]
    hidden = jnp.concatenate(
        [
            (normed * gain + mod_ref[0:1]).astype(BF),
            (dnormed * gain + normed * mod_ref[4:5] + mod_ref[3:4]).astype(BF),
        ],
        axis=0,
    )
    factor = HD ** (-0.5)
    for g in range(groups):
        pltpu.make_async_copy(w_in.at[g], w_in.at[g], sems.at[g]).wait()
        proj = dot(hidden, w_in[g].reshape(width, cols)).astype(BF)
        for i in range(part // HD):
            q = proj[:, i * HD : (i + 1) * HD]
            k = proj[:, part + i * HD : part + (i + 1) * HD]
            u = proj[:, 2 * part + i * HD : 2 * part + (i + 1) * HD]
            q, dq, k, dk = (q[:length], q[length:], k[:length], k[length:])
            sc = dot(q, k, ((1,), (1,))) * factor
            e = jnp.exp(sc - jnp.max(sc, -1, keepdims=True))
            p = e / jnp.sum(e, -1, keepdims=True)
            dsc = (
                dot(
                    jnp.concatenate([dq, q], 1), jnp.concatenate([k, dk], 1), ((1,), (1,))
                )
                * factor
            )
            dp = p * (dsc - jnp.sum(p * dsc, -1, keepdims=True))
            pb, dpb = (p.astype(BF), dp.astype(BF))
            lanes = pl.ds(g * part + i * HD, HD)
            heads[0:length, lanes] = dot(pb, u[:length]).astype(BF)
            heads[length:, lanes] = dot(jnp.concatenate([dpb, pb], 1), u).astype(BF)
    pltpu.make_async_copy(w_proj, w_proj, sems.at[groups]).wait()
    both = dot(heads[...], w_proj[...].reshape(width, width))
    gate, dgate = (mod_ref[2:3], mod_ref[5:6])
    a, da = (both[:length], both[length:])
    out_ref[:length] = (x + gate * a).astype(BF)
    out_ref[length:] = (v + gate * da + dgate * a).astype(BF)


def layer(xv, mod, w_long, w_short):
    ys, z_hi, groups, _, lanes = w_long.shape
    width = xv.shape[1]
    part = width // groups
    cols = lanes - part
    rows = w_long.shape[3] + w_short.shape[3]
    vmem = pl.BlockSpec(memory_space=pltpu.VMEM)
    hbm = pl.BlockSpec(memory_space=pl.ANY)
    return pl.pallas_call(
        layer_kernel,
        out_shape=jax.ShapeDtypeStruct(xv.shape, BF),
        in_specs=[vmem, vmem, hbm, hbm],
        out_specs=vmem,
        scratch_shapes=[
            pltpu.VMEM((groups, z_hi, ys, rows, cols), BF),
            pltpu.VMEM((z_hi, ys, rows, width), BF),
            pltpu.VMEM(xv.shape, BF),
            pltpu.SemaphoreType.DMA((groups + 1,)),
        ],
        compiler_params=pltpu.CompilerParams(vmem_limit_bytes=48 * 1024 * 1024),
        name="layer",
    )(xv, mod, w_long, w_short)


def body(x_in, tangent_in, timesteps, mod_table, w_qkv, w_out):
    count, length, part = x_in.shape
    groups = lax.axis_size("zl")
    sections = lax.axis_size("x") * lax.axis_size("c")
    section = lax.axis_index(("x", "c"))
    own = lax.axis_index("zl")
    width = part * groups

    share = jnp.concatenate([w_qkv[0].reshape(-1, 3 * part), w_out[0]], axis=1)
    long, short = (share[:LONG], share[LONG:])
    w_long = lax.all_gather(lax.all_gather(long, ("zh", "zl")), "y")
    w_short = lax.all_gather(lax.all_gather(short, "y"), ("zh", "zl"))
    w_long = w_long.reshape(-1, w_long.shape[1] // groups, groups, *long.shape)
    w_short = w_short.reshape(-1, groups, w_short.shape[1], *short.shape)

    level = lax.dynamic_index_in_dim(timesteps, own, 0, keepdims=False)
    mod = lax.dynamic_index_in_dim(mod_table[0], level, 0, keepdims=False).astype(F32)

    both = jnp.stack([x_in, tangent_in], axis=1)
    both = lax.all_to_all(both, "zl", 0, 0)
    here = both.transpose(1, 2, 0, 3).reshape(2 * length, width)

    result = jnp.zeros_like(here)
    for t in range(sections):
        result = lax.cond(
            section == t,
            lambda held, at: layer(at, mod, w_long, w_short),
            lambda held, at: held,
            result,
            here,
        )
        if t < sections - 1:
            here = lax.ppermute(result, ("x", "c"), [(t, t + 1)])

    result = result.reshape(2, length, groups, part).transpose(2, 0, 1, 3)
    result = lax.all_to_all(result, "zl", 0, 0)
    return (result[None, :, 0], result[None, :, 1])


def solution(mesh):
    tensor = mesh.shape["tensor"]
    ys = 4
    fine = Mesh(
        np.asarray(mesh.devices).reshape(mesh.shape["dp"] // ys, ys, -1, 2, tensor),
        ("zh", "y", "x", "c", "zl"),
    )
    dp, section = (("zh", "y"), ("x", "c"))
    in_specs = (
        P(dp, None, "zl"),
        P(dp, None, "zl"),
        P(dp),
        P(section, None, None, None),
        P(section, dp, None, "zl"),
        P(section, dp, "zl"),
    )
    out_specs = (P(section, dp, None, "zl"), P(section, dp, None, "zl"))
    return jax.shard_map(body, mesh=fine, in_specs=in_specs, out_specs=out_specs, check_vma=False)
```

time: 1060 us -> 477 us (0.45)
  blocking collectives: 536 us -> 27.8 us
  other arithmetic: 47.4 us -> 3.24 us
  local copies, waits for them, and re-layouts: 41.7 us -> 3.19 us
  matrix products: 25.2 us -> 0 us
  loops' own time: 2.04 us -> 24.3 us
  waiting for transfers between devices: 355 us -> 374 us
  starting transfers between devices: 25.8 us -> 9.17 us
  Pallas kernels: 0 us -> 11.7 us
    all_gather x44 -> x1, blocking collectives: 536 us -> 11.6 us  [body(): w_short = lax.all_gather(lax.all_gather(short, 'y'), ('zh', 'zl'))]
    all_gather x2 -> x3, waiting for transfers between devices: 191 us -> 263 us  [the longest x2 187 us: body(): w_long = lax.all_gather(lax.all_gather(long, ('zh', 'zl')), 'y')]
    ppermute x20 -> x7, waiting for transfers between devices: 162 us -> 102 us  [body(): here = lax.ppermute(result, ('x', 'c'), [(t, t + 1)])]
    dot_general x37 -> x0, matrix products: 24 us -> none  [the longest x4 9.72 us: section_layer(): jnp.dot(hidden_in, w_in, preferred_element_type=jnp.float32)]
    another operation x34 -> x8, loops' own time: 2.04 us -> 24.3 us  [body(): lax.cond(section == t, lambda held, at: layer(at, mod, w_long, w_short),...]
    select_n x22 -> x0, other arithmetic: 20.8 us -> none  [the longest x11 10.5 us: run_tick(): jnp.where(first_section, lax.dynamic_index_in_dim(x_in, clipped, 0, keepd...]
    ppermute x20 -> x7, starting transfers between devices: 25.7 us -> 5.56 us  [body(): here = lax.ppermute(result, ('x', 'c'), [(t, t + 1)])]
    all_to_all x0 -> x1, blocking collectives: none -> 16.3 us  [body(): result = lax.all_to_all(result, 'zl', 0, 0)]
  transfers between devices with their start and end apart: 22 -> 11, of which waited for: 22 -> 5; matrix products, arithmetic and copies ran while one was open for 1% -> 1% of each run, Pallas kernels for 0% -> 0%
where the time goes in v1:
time: 477 us; the launch traced here: 470 us
  waiting for transfers between devices  374 us (78%)
  blocking collectives  27.8 us (6%)
  loops' own time  24.3 us (5%)
  between operations  16.5 us (3%)
  Pallas kernels  11.7 us (2%)
  starting transfers between devices  9.17 us (2%)
    all_gather x2, waiting for transfers between devices, body(): w_long = lax.all_gather(lax.all_gather(long, ('zh', 'zl')), 'y')  187 us
    ppermute x7, waiting for transfers between devices, body(): here = lax.ppermute(result, ('x', 'c'), [(t, t + 1)])  102 us
    all_gather x1, waiting for transfers between devices, body(): w_short = lax.all_gather(lax.all_gather(short, 'y'), ('zh', 'zl'))  75.2 us
    another operation x8, loops' own time, body(): lax.cond(section == t, lambda held, at: layer(at, mod, w_long, w_short),...  24.3 us
    all_to_all x1, blocking collectives, body(): result = lax.all_to_all(result, 'zl', 0, 0)  16.3 us
    pallas_call x1, Pallas kernels, layer(): pl.pallas_call(layer_kernel, out_shape=jax.ShapeDtypeStruct(xv.shape, BF)...  11.7 us
    all_gather x1, blocking collectives, body(): w_short = lax.all_gather(lax.all_gather(short, 'y'), ('zh', 'zl'))  11.6 us
    all_to_all x1, waiting for transfers between devices, body(): both = lax.all_to_all(both, 'zl', 0, 0)  9.54 us
  transfers between devices with their start and end apart: 11, of which 5 were waited for; matrix products, arithmetic and copies ran while one was open for 1% of the time, Pallas kernels for 0%

profile of v1, /device:TPU:7, one launch (start us, length us, event | category | flops | bytes accessed | tf_op | source)
XLA Modules:
  0.0 470.2 jit_solution(4038428442724758503)
XLA Ops:
  7.2 1.2 copy.18
  8.5 1.5 fusion
  10.1 0.8 pad_maximum_fusion.1
  10.8 11.6 %all-gather.2 = bf16[128,1536]{1,0:T(8,128)(2,1)} all-gather(bf16[32,1536]{1,0:T(8,128)(2,1)S(1)} %pad_maximum_fusion.1), channel_id=4, replica_groups=mesh['zh'=4,'y'=4,'x'=4,'c'=2,'zl'=4] {'y'}, dimensions={0}, use_global_device_ids=true | all-gather | bytes 491520 | tf_op jit(solution)/shard_map/all_gather | solution.py:133
  22.5 60.3 %all-gather.8.cloned.1.call-done = bf16[1024,1536]{1,0:T(8,128)(2,1)} async-done(((bf16[64,1536]{1,0:T(8,128)(2,1)}), bf16[1024,1536]{1,0:T(8,128)(2,1)}) %all-gather.8.cloned.1.call-update) | async-done | bytes 3145744 | tf_op jit(solution)/shard_map/all_gather | solution.py:132
  82.8 1.0 pad_maximum_fusion
  83.8 3.5 all-to-all-start
  89.9 9.5 %all-to-all-done = bf16[4,2,128,384]{3,2,1,0:T(8,128)(2,1)S(1)} async-done(((bf16[4,2,128,384]{3,2,1,0:T(8,128)(2,1)}), bf16[4,2,128,384]{3,2,1,0:T(8,128)(2,1)S(1)}, u32[]{:S(2)}, u32[]{:S(2)}) %all-to-all-start) | async-done | bytes 786464 | tf_op jit(solution)/shard_map/all_to_all | solution.py:141
  99.4 75.2 %all-gather.12.cloned.1.call-done = bf16[64,32,1536]{2,1,0:T(8,128)(2,1)} async-done(((bf16[4,32,1536]{2,1,0:T(8,128)(2,1)}), bf16[64,32,1536]{2,1,0:T(8,128)(2,1)}) %all-gather.12.cloned.1.call-update) | async-done | bytes 6291472 | tf_op jit(solution)/shard_map/all_gather | solution.py:133
  174.6 127.1 %all-gather.10.cloned.1.call-done = bf16[64,64,1536]{2,1,0:T(8,128)(2,1)} async-done(((bf16[16,64,1536]{2,1,0:T(8,128)(2,1)}), bf16[64,64,1536]{2,1,0:T(8,128)(2,1)}) %all-gather.10.cloned.1.call-update) | async-done | bytes 12582928 | tf_op jit(solution)/shard_map/all_gather | solution.py:132
  301.8 0.7 collective-permute-start
  302.7 0.7 collective-permute-start.1
  303.5 4.7 %conditional.10 = (bf16[256,1536]{1,0:T(8,128)(2,1)S(1)}) conditional(s32[]{:T(128)} %convert_element_type.35, bf16[256,1536]{1,0:T(8,128)(2,1)S(1)} %get-tuple-element.139, (bf16[256,1536]{1,0:T(8,128)(2,1)S(1)}, f32[6,1536]{1,0:T(8,128)S(1)}, bf16[4,4,4,64,1536]{4,3,2,1,0:T(8,128)(2,1)}, bf16[4,4,4,32,1536]{4,3,2,1,0:T(8,128)(2,1)}) %tuple.101), branch_computations={%region_4.5_spmd, %region_5.6_spmd} | conditional | bytes 8 | solution.py:146
  308.2 0.7 collective-permute-start.2
  309.0 4.9 %conditional.11 = (bf16[256,1536]{1,0:T(8,128)(2,1)S(1)}) conditional(s32[]{:T(128)} %convert_element_type.34, bf16[256,1536]{1,0:T(8,128)(2,1)S(1)} %get-tuple-element.140, (bf16[256,1536]{1,0:T(8,128)(2,1)S(1)}, f32[6,1536]{1,0:T(8,128)S(1)}, bf16[4,4,4,64,1536]{4,3,2,1,0:T(8,128)(2,1)}, bf16[4,4,4,32,1536]{4,3,2,1,0:T(8,128)(2,1)}) %tuple.102), branch_computations={%region_6.7_spmd, %region_7.8_spmd} | conditional | bytes 8 | solution.py:146
  314.6 4.7 conditional.12
  320.0 4.7 conditional.13
  325.5 4.7 %conditional.14 = (bf16[256,1536]{1,0:T(8,128)(2,1)S(1)}) conditional(s32[]{:T(128)} %convert_element_type.31, bf16[256,1536]{1,0:T(8,128)(2,1)S(1)} %get-tuple-element.143, (bf16[256,1536]{1,0:T(8,128)(2,1)S(1)}, f32[6,1536]{1,0:T(8,128)S(1)}, bf16[4,4,4,64,1536]{4,3,2,1,0:T(8,128)(2,1)}, bf16[4,4,4,32,1536]{4,3,2,1,0:T(8,128)(2,1)}) %tuple.105), branch_computations={%region_12.13_spmd, %region_13.14_spmd} | conditional | bytes 8 | solution.py:146
  330.2 1.3 collective-permute-start.6
  331.5 102.2 %collective-permute-done.6 = bf16[256,1536]{1,0:T(8,128)(2,1)S(1)} collective-permute-done((bf16[256,1536]{1,0:T(8,128)(2,1)S(1)}, bf16[256,1536]{1,0:T(8,128)(2,1)S(1)}, u32[]{:S(2)}, u32[]{:S(2)}) %collective-permute-start.6) | collective-permute-done | bytes 786464 | tf_op jit(solution)/shard_map/ppermute | solution.py:154
  433.7 11.9 %conditional.15 = (bf16[256,1536]{1,0:T(8,128)(2,1)S(1)}) conditional(s32[]{:T(128)} %convert_element_type.30, bf16[256,1536]{1,0:T(8,128)(2,1)S(1)} %get-tuple-element.144, (bf16[256,1536]{1,0:T(8,128)(2,1)S(1)}, f32[6,1536]{1,0:T(8,128)S(1)}, bf16[4,4,4,64,1536]{4,3,2,1,0:T(8,128)(2,1)}, bf16[4,4,4,32,1536]{4,3,2,1,0:T(8,128)(2,1)}) %tuple.106), branch_computations={%region_14.15_spmd, %region_15.16_spmd} | conditional | bytes 8 | solution.py:146
  434.0 11.7 %layer.15 = bf16[256,1536]{1,0:T(8,128)(2,1)S(1)} custom-call(bf16[256,1536]{1,0:T(8,128)(2,1)S(1)} %get-tuple-element.123.xv_ref, f32[6,1536]{1,0:T(8,128)S(1)} %get-tuple-element.124.mod_ref, bf16[4,4,4,64,1536]{4,3,2,1,0:T(8,128)(2,1)} %get-tuple-element.125.wl_ref, bf16[4,4,4,32,1536]{4,3,2,1,0:T(8,128)(2,1)} %get-tuple-element.126.ws_ref), custom_call_target="tpu_custom_call" | custom-call | tf_op jit(solution)/shard_map/cond/branch_1_fun/layer/pallas_call | solution.py:106
  445.9 16.3 %all_to_all.10 = bf16[4,2,128,384]{3,2,1,0:T(8,128)(2,1)S(1)} all-to-all(bf16[4,2,128,384]{3,2,1,0:T(8,128)(2,1)S(1)} %copy.20), channel_id=1, replica_groups=mesh['zh'=4,'y'=4,'x'=4,'c'=2,'zl'=4] {'zl'}, dimensions={0} | all-to-all | bytes 1572864 | tf_op jit(solution)/shard_map/all_to_all | solution.py:157
  462.2 1.0 slice_bitcast_fusion
  (32 shorter events, 3.6 us)
Async XLA Ops:
  7.2 82.6 %copy-start = (bf16[1,64,6,1536]{3,1,2,0:T(8,128)(2,1)S(1)}, bf16[1,64,6,1536]{3,1,2,0:T(8,128)(2,1)}, u32[]{:S(2)}) copy-start(bf16[1,64,6,1536]{3,1,2,0:T(8,128)(2,1)} %param.25) | copy-start | bytes 3538948
  7.2 75.6 %copy-start.1 = (bf16[4,128,384]{2,1,0:T(8,128)(2,1)S(1)}, bf16[4,128,384]{2,1,0:T(8,128)(2,1)}, u32[]{:S(2)}) copy-start(bf16[4,128,384]{2,1,0:T(8,128)(2,1)} %param.23) | copy-start | bytes 1179652
  7.2 75.6 %copy-start.2 = (bf16[4,128,384]{2,1,0:T(8,128)(2,1)S(1)}, bf16[4,128,384]{2,1,0:T(8,128)(2,1)}, u32[]{:S(2)}) copy-start(bf16[4,128,384]{2,1,0:T(8,128)(2,1)} %param.22) | copy-start | bytes 1179652
  7.2 75.5 %all-gather.8.cloned.1.call-start = ((), (), s32[]{:S(2)}) async-start(), calls=%async_computation.2 | async-start | bytes 3342336 | tf_op jit(solution)/shard_map/all_gather | solution.py:132
  10.0 164.6 %all-gather.12.cloned.1.call-start = ((), (), s32[]{:S(2)}) async-start(), calls=%async_computation.4 | async-start | bytes 6684672 | tf_op jit(solution)/shard_map/all_gather | solution.py:133
  22.4 279.3 %all-gather.10.cloned.1.call-start = ((), (), s32[]{:S(2)}) async-start(), calls=%async_computation.3 | async-start | bytes 15728640 | tf_op jit(solution)/shard_map/all_gather | solution.py:132
  82.7 4.5 copy-start.3
  83.8 15.7 %all-to-all-start = ((bf16[4,2,128,384]{3,2,1,0:T(8,128)(2,1)}), bf16[4,2,128,384]{3,2,1,0:T(8,128)(2,1)S(1)}, u32[]{:S(2)}, u32[]{:S(2)}) async-start(bf16[4,2,128,384]{3,2,1,0:T(8,128)(2,1)} %pad_maximum_fusion), calls=%async_computation | async-start | bytes 1572864 | tf_op jit(solution)/shard_map/all_to_all | solution.py:141
  301.8 0.7 collective-permute-start
  302.7 0.7 collective-permute-start.1
  308.2 0.7 collective-permute-start.2
  313.9 0.7 collective-permute-start.3
  319.3 0.7 collective-permute-start.4
  324.7 0.7 collective-permute-start.5
  330.2 103.5 %collective-permute-start.6 = (bf16[256,1536]{1,0:T(8,128)(2,1)S(1)}, bf16[256,1536]{1,0:T(8,128)(2,1)S(1)}, u32[]{:S(2)}, u32[]{:S(2)}) collective-permute-start(bf16[256,1536]{1,0:T(8,128)(2,1)S(1)} %get-tuple-element.144), channel_id=1, source_target_pairs={{24,28},{25,29},{26,30},{27,31},{56,60},{57,61},{58,62},{59,63},{8... | collective-permute-start | bytes 2359304 | tf_op jit(solution)/shard_map/ppermute | solution.py:154
Sparse Core Ops, SparseCore 0:
  10.7 71.9 all-gather.7
  84.8 89.8 all-gather.11
  176.8 124.9 all-gather.9

commit v2 on v1

--- a/solution.py
+++ b/solution.py
@@ -18,31 +18,50 @@
     return lax.dot_general(a, b, (dims, ((), ())), preferred_element_type=F32)
 
 
-def layer_kernel(xv_ref, mod_ref, wl_ref, ws_ref, out_ref, w_in, w_proj, heads, sems):
+def shift(block, axis, by):
+    size = lax.axis_size(axis)
+    return lax.ppermute(block, axis, [(i, (i + by) % size) for i in range(size)])
+
+
+def layer_kernel(
+    y_ref, xv_ref, mod_ref, own_ref, prev_ref, next_ref, far_a_ref, far_b_ref, short_ref,
+    out_ref, w_in, w_proj, heads, sems,
+):
     groups, z_hi, ys, rows, cols = w_in.shape
     width = xv_ref.shape[1]
     length = xv_ref.shape[0] // 2
     part = width // groups
+    half = z_hi // 2
+    y = y_ref[0]
+    before, after, far = (lax.rem(y + ys + d, ys) for d in (-1, 1, 2))
+    every = pl.ds(0, z_hi)
+    sources = (
+        (own_ref, every, y),
+        (prev_ref, every, before),
+        (next_ref, every, after),
+        (far_a_ref, pl.ds(0, half), far),
+        (far_b_ref, pl.ds(half, half), far),
+    )
     for g in range(groups):
-        for y in range(ys):
+        for ref, z, at in sources:
             pltpu.make_async_copy(
-                wl_ref.at[y, :, g, :, pl.ds(0, cols)], w_in.at[g, :, y, pl.ds(0, LONG)], sems.at[g]
+                ref.at[:, g, :, pl.ds(0, cols)], w_in.at[g, z, at, pl.ds(0, LONG)], sems.at[g]
             ).start()
         pltpu.make_async_copy(
-            ws_ref.at[:, g, :, :, pl.ds(0, cols)],
+            short_ref.at[:, g, :, :, pl.ds(0, cols)],
             w_in.at[g, :, :, pl.ds(LONG, rows - LONG)],
             sems.at[g],
         ).start()
     for g in range(groups):
         lanes = pl.ds(g * part, part)
-        for y in range(ys):
+        for ref, z, at in sources:
             pltpu.make_async_copy(
-                wl_ref.at[y, :, g, :, pl.ds(cols, part)],
-                w_proj.at[:, y, pl.ds(0, LONG), lanes],
+                ref.at[:, g, :, pl.ds(cols, part)],
+                w_proj.at[z, at, pl.ds(0, LONG), lanes],
                 sems.at[groups],
             ).start()
         pltpu.make_async_copy(
-            ws_ref.at[:, g, :, :, pl.ds(cols, part)],
+            short_ref.at[:, g, :, :, pl.ds(cols, part)],
             w_proj.at[:, :, pl.ds(LONG, rows - LONG), lanes],
             sems.at[groups],
         ).start()
@@ -95,18 +114,18 @@
     out_ref[length:] = (v + gate * da + dgate * a).astype(BF)
 
 
-def layer(xv, mod, w_long, w_short):
-    ys, z_hi, groups, _, lanes = w_long.shape
+def layer(y, xv, mod, weights):
+    z_hi, groups, ys, rest, lanes = weights[-1].shape
     width = xv.shape[1]
     part = width // groups
     cols = lanes - part
-    rows = w_long.shape[3] + w_short.shape[3]
+    rows = LONG + rest
     vmem = pl.BlockSpec(memory_space=pltpu.VMEM)
     hbm = pl.BlockSpec(memory_space=pl.ANY)
     return pl.pallas_call(
         layer_kernel,
         out_shape=jax.ShapeDtypeStruct(xv.shape, BF),
-        in_specs=[vmem, vmem, hbm, hbm],
+        in_specs=[pl.BlockSpec(memory_space=pltpu.SMEM), vmem, vmem] + [hbm] * len(weights),
         out_specs=vmem,
         scratch_shapes=[
             pltpu.VMEM((groups, z_hi, ys, rows, cols), BF),
@@ -116,7 +135,7 @@
         ],
         compiler_params=pltpu.CompilerParams(vmem_limit_bytes=48 * 1024 * 1024),
         name="layer",
-    )(xv, mod, w_long, w_short)
+    )(y, xv, mod, *weights)
 
 
 def body(x_in, tangent_in, timesteps, mod_table, w_qkv, w_out):
@@ -129,10 +148,17 @@
 
     share = jnp.concatenate([w_qkv[0].reshape(-1, 3 * part), w_out[0]], axis=1)
     long, short = (share[:LONG], share[LONG:])
-    w_long = lax.all_gather(lax.all_gather(long, ("zh", "zl")), "y")
-    w_short = lax.all_gather(lax.all_gather(short, "y"), ("zh", "zl"))
-    w_long = w_long.reshape(-1, w_long.shape[1] // groups, groups, *long.shape)
-    w_short = w_short.reshape(-1, groups, w_short.shape[1], *short.shape)
+    z = ("zh", "zl")
+    mine = lax.all_gather(long, z)
+    short = lax.all_gather(lax.all_gather(short, "y"), z)
+    zs = mine.shape[0]
+    from_prev, from_next = (shift(mine, "y", 1), shift(mine, "y", -1))
+    far_a, far_b = (shift(from_prev[: zs // 2], "y", 1), shift(from_next[zs // 2 :], "y", -1))
+    weights = [
+        w.reshape(w.shape[0] // groups, groups, *w.shape[1:])
+        for w in (mine, from_prev, from_next, far_a, far_b, short)
+    ]
+    y = lax.axis_index("y").reshape(1)
 
     level = lax.dynamic_index_in_dim(timesteps, own, 0, keepdims=False)
     mod = lax.dynamic_index_in_dim(mod_table[0], level, 0, keepdims=False).astype(F32)
@@ -145,7 +171,7 @@
     for t in range(sections):
         result = lax.cond(
             section == t,
-            lambda held, at: layer(at, mod, w_long, w_short),
+            lambda held, at: layer(y, at, mod, weights),
             lambda held, at: held,
             result,
             here,

time: 477 us -> 388 us (0.81)
  the two profiles are of different devices: /device:TPU:7 before, /device:TPU:31 now
where the time goes in v2:
time: 388 us; the launch traced here: 381 us
  waiting for transfers between devices  265 us (68%)
  starting transfers between devices  25.8 us (7%)
  blocking collectives  25.6 us (7%)
  loops' own time  20.2 us (5%)
  between operations  16.7 us (4%)
  Pallas kernels  13.6 us (4%)
  local copies, waits for them, and re-layouts  11.1 us (3%)
    ppermute x7, waiting for transfers between devices, body(): here = lax.ppermute(result, ('x', 'c'), [(t, t + 1)])  128 us
    ppermute x4, waiting for transfers between devices, shift(): lax.ppermute(block, axis, [(i, (i + by) % size) for i in range(size)])  75.6 us
    all_gather x1, waiting for transfers between devices, body(): mine = lax.all_gather(long, z)  62 us
    another operation x8, loops' own time, body(): lax.cond(section == t, lambda held, at: layer(y, at, mod, weights), lambd...  20.2 us
    all_to_all x1, blocking collectives, body(): result = lax.all_to_all(result, 'zl', 0, 0)  15.2 us
    pallas_call x1, Pallas kernels, layer(): pl.pallas_call(layer_kernel, out_shape=jax.ShapeDtypeStruct(xv.shape, BF)...  13.6 us
    ppermute x7, starting transfers between devices, body(): here = lax.ppermute(result, ('x', 'c'), [(t, t + 1)])  10.9 us
    ppermute x4, starting transfers between devices, shift(): lax.ppermute(block, axis, [(i, (i + by) % size) for i in range(size)])  10.7 us
  transfers between devices with their start and end apart: 14, of which 5 were waited for; matrix products, arithmetic and copies ran while one was open for 2% of the time, Pallas kernels for 0%

profile of v2, /device:TPU:31, one launch (start us, length us, event | category | flops | bytes accessed | tf_op | source)
XLA Modules:
  0.0 380.7 jit_solution(12112251941434261273)
XLA Ops:
  10.1 10.4 %all-gather.1 = bf16[128,1536]{1,0:T(8,128)(2,1)} all-gather(bf16[32,1536]{1,0:T(8,128)(2,1)S(1)} %pad_maximum_fusion.1), channel_id=3, replica_groups=mesh['zh'=4,'y'=4,'x'=4,'c'=2,'zl'=4] {'y'}, dimensions={0}, use_global_device_ids=true | all-gather | bytes 491520 | tf_op jit(solution)/shard_map/all_gather | solution.py:153
  20.5 62.0 %all-gather.6.cloned.1.call-done = bf16[1024,1536]{1,0:T(8,128)(2,1)} async-done(((bf16[64,1536]{1,0:T(8,128)(2,1)}), bf16[1024,1536]{1,0:T(8,128)(2,1)}) %all-gather.6.cloned.1.call-update) | async-done | bytes 3145744 | tf_op jit(solution)/shard_map/all_gather | solution.py:152
  82.5 2.1 collective-permute-start
  84.6 3.2 collective-permute-start.1
  88.8 4.2 %all-to-all-start = ((bf16[4,2,128,384]{3,2,1,0:T(8,128)(2,1)}), bf16[4,2,128,384]{3,2,1,0:T(8,128)(2,1)}, u32[]{:S(2)}, u32[]{:S(2)}) async-start(bf16[4,2,128,384]{3,2,1,0:T(8,128)(2,1)} %pad_maximum_fusion), calls=%async_computation | async-start | bytes 1572864 | tf_op jit(solution)/shard_map/all_to_all | solution.py:167
  92.9 52.1 %collective-permute-done = bf16[16,64,1536]{2,1,0:T(8,128)(2,1)} collective-permute-done((bf16[16,64,1536]{2,1,0:T(8,128)(2,1)}, bf16[16,64,1536]{2,1,0:T(8,128)(2,1)}, u32[]{:S(2)}, u32[]{:S(2)}) %collective-permute-start) | collective-permute-done | bytes 3145760 | tf_op jit(solution)/shard_map/ppermute | solution.py:23
  145.1 2.7 slice.26
  147.7 3.4 collective-permute-start.2
  151.2 2.7 slice.27
  153.9 2.0 collective-permute-start.3
  158.5 19.4 %collective-permute-done.2 = bf16[8,64,1536]{2,1,0:T(8,128)(2,1)S(1)} collective-permute-done((bf16[8,64,1536]{2,1,0:T(8,128)(2,1)}, bf16[8,64,1536]{2,1,0:T(8,128)(2,1)S(1)}, u32[]{:S(2)}, u32[]{:S(2)}) %collective-permute-start.2) | collective-permute-done | bytes 1572896 | tf_op jit(solution)/shard_map/ppermute | solution.py:23
  177.9 4.1 %collective-permute-done.3 = bf16[8,64,1536]{2,1,0:T(8,128)(2,1)} collective-permute-done((bf16[8,64,1536]{2,1,0:T(8,128)(2,1)}, bf16[8,64,1536]{2,1,0:T(8,128)(2,1)}, u32[]{:S(2)}, u32[]{:S(2)}) %collective-permute-start.3) | collective-permute-done | bytes 1572896 | tf_op jit(solution)/shard_map/ppermute | solution.py:23
  184.7 1.6 collective-permute-start.5
  186.3 3.9 %conditional.10 = (bf16[256,1536]{1,0:T(8,128)(2,1)}) conditional(s32[]{:T(128)} %convert_element_type.35, bf16[256,1536]{1,0:T(8,128)(2,1)} %get-tuple-element.264, (s32[1]{0:T(128)}, bf16[256,1536]{1,0:T(8,128)(2,1)}, f32[6,1536]{1,0:T(8,128)S(1)}, bf16[4,4,64,1536]{3,2,1,0:T(8,128)(2,1)}, bf16[4,4,64,1536]{3,2,1,0:T(8,128)(2,1)}, ...), branch_computations={%region_4.5_spmd, %region_5.6_spmd} | conditional | bytes 8 | solution.py:172
  190.3 1.6 collective-permute-start.6
  191.9 4.1 %conditional.11 = (bf16[256,1536]{1,0:T(8,128)(2,1)}) conditional(s32[]{:T(128)} %convert_element_type.34, bf16[256,1536]{1,0:T(8,128)(2,1)} %get-tuple-element.265, (s32[1]{0:T(128)}, bf16[256,1536]{1,0:T(8,128)(2,1)}, f32[6,1536]{1,0:T(8,128)S(1)}, bf16[4,4,64,1536]{3,2,1,0:T(8,128)(2,1)}, bf16[4,4,64,1536]{3,2,1,0:T(8,128)(2,1)}, ...), branch_computations={%region_6.7_spmd, %region_7.8_spmd} | conditional | bytes 8 | solution.py:172
  197.6 3.8 %conditional.12 = (bf16[256,1536]{1,0:T(8,128)(2,1)}) conditional(s32[]{:T(128)} %convert_element_type.33, bf16[256,1536]{1,0:T(8,128)(2,1)} %get-tuple-element.266, (s32[1]{0:T(128)}, bf16[256,1536]{1,0:T(8,128)(2,1)}, f32[6,1536]{1,0:T(8,128)S(1)}, bf16[4,4,64,1536]{3,2,1,0:T(8,128)(2,1)}, bf16[4,4,64,1536]{3,2,1,0:T(8,128)(2,1)}, ...), branch_computations={%region_8.9_spmd, %region_9.10_spmd} | conditional | bytes 8 | solution.py:172
  203.1 3.9 %conditional.13 = (bf16[256,1536]{1,0:T(8,128)(2,1)}) conditional(s32[]{:T(128)} %convert_element_type.32, bf16[256,1536]{1,0:T(8,128)(2,1)} %get-tuple-element.267, (s32[1]{0:T(128)}, bf16[256,1536]{1,0:T(8,128)(2,1)}, f32[6,1536]{1,0:T(8,128)S(1)}, bf16[4,4,64,1536]{3,2,1,0:T(8,128)(2,1)}, bf16[4,4,64,1536]{3,2,1,0:T(8,128)(2,1)}, ...), branch_computations={%region_10.11_spmd, %region_11.12_spmd} | conditional | bytes 8 | solution.py:172
  208.6 3.9 %conditional.14 = (bf16[256,1536]{1,0:T(8,128)(2,1)}) conditional(s32[]{:T(128)} %convert_element_type.31, bf16[256,1536]{1,0:T(8,128)(2,1)} %get-tuple-element.268, (s32[1]{0:T(128)}, bf16[256,1536]{1,0:T(8,128)(2,1)}, f32[6,1536]{1,0:T(8,128)S(1)}, bf16[4,4,64,1536]{3,2,1,0:T(8,128)(2,1)}, bf16[4,4,64,1536]{3,2,1,0:T(8,128)(2,1)}, ...), branch_computations={%region_12.13_spmd, %region_13.14_spmd} | conditional | bytes 8 | solution.py:172
  213.8 127.6 %collective-permute-done.10 = bf16[256,1536]{1,0:T(8,128)(2,1)} collective-permute-done((bf16[256,1536]{1,0:T(8,128)(2,1)}, bf16[256,1536]{1,0:T(8,128)(2,1)}, u32[]{:S(2)}, u32[]{:S(2)}) %collective-permute-start.10) | collective-permute-done | bytes 786464 | tf_op jit(solution)/shard_map/ppermute | solution.py:180
  341.4 13.9 %conditional.15 = (bf16[256,1536]{1,0:T(8,128)(2,1)}) conditional(s32[]{:T(128)} %convert_element_type.30, bf16[256,1536]{1,0:T(8,128)(2,1)} %get-tuple-element.269, (s32[1]{0:T(128)}, bf16[256,1536]{1,0:T(8,128)(2,1)}, f32[6,1536]{1,0:T(8,128)S(1)}, bf16[4,4,64,1536]{3,2,1,0:T(8,128)(2,1)}, bf16[4,4,64,1536]{3,2,1,0:T(8,128)(2,1)}, ...), branch_computations={%region_14.15_spmd, %region_15.16_spmd} | conditional | bytes 8 | solution.py:172
  341.7 13.6 %layer.15 = bf16[256,1536]{1,0:T(8,128)(2,1)} custom-call(s32[1]{0:T(128)} %get-tuple-element.238.y_ref, bf16[256,1536]{1,0:T(8,128)(2,1)} %get-tuple-element.239.xv_ref, f32[6,1536]{1,0:T(8,128)S(1)} %get-tuple-element.240.mod_ref, bf16[4,4,64,1536]{3,2,1,0:T(8,128)(2,1)} %get-tuple-element.241.own_ref, ...), custom_call_target="tpu_custom_call" | custom-call | tf_op jit(solution)/shard_map/cond/branch_1_fun/layer/pallas_call | solution.py:125
  355.3 1.8 reshape.43
  357.1 15.2 %all_to_all.10 = bf16[4,2,128,384]{3,2,1,0:T(8,128)(2,1)S(1)} all-to-all(bf16[4,2,128,384]{3,2,1,0:T(8,128)(2,1)S(1)} %copy.20), channel_id=1, replica_groups=mesh['zh'=4,'y'=4,'x'=4,'c'=2,'zl'=4] {'zl'}, dimensions={0} | all-to-all | bytes 1572864 | tf_op jit(solution)/shard_map/all_to_all | solution.py:183
  (41 shorter events, 15.4 us)
Async XLA Ops:
  7.2 151.2 %copy-start = (bf16[1,64,6,1536]{3,1,2,0:T(8,128)(2,1)S(1)}, bf16[1,64,6,1536]{3,1,2,0:T(8,128)(2,1)}, u32[]{:S(2)}) copy-start(bf16[1,64,6,1536]{3,1,2,0:T(8,128)(2,1)} %param.25) | copy-start | bytes 3538948
  7.2 2.9 copy-start.4
  7.2 80.6 %copy-start.3 = (bf16[4,128,384]{2,1,0:T(8,128)(2,1)S(1)}, bf16[4,128,384]{2,1,0:T(8,128)(2,1)}, u32[]{:S(2)}) copy-start(bf16[4,128,384]{2,1,0:T(8,128)(2,1)} %param.22) | copy-start | bytes 1179652
  7.2 80.6 %copy-start.2 = (bf16[4,128,384]{2,1,0:T(8,128)(2,1)S(1)}, bf16[4,128,384]{2,1,0:T(8,128)(2,1)}, u32[]{:S(2)}) copy-start(bf16[4,128,384]{2,1,0:T(8,128)(2,1)} %param.23) | copy-start | bytes 1179652
  7.2 75.2 %all-gather.6.cloned.1.call-start = ((), (), s32[]{:S(2)}) async-start(), calls=%async_computation.2 | async-start | bytes 3342336 | tf_op jit(solution)/shard_map/all_gather | solution.py:152
  10.0 172.0 %all-gather.8.cloned.1.call-start = ((), (), s32[]{:S(2)}) async-start(), calls=%async_computation.3 | async-start | bytes 6684672 | tf_op jit(solution)/shard_map/all_gather | solution.py:153
  82.5 62.6 %collective-permute-start = (bf16[16,64,1536]{2,1,0:T(8,128)(2,1)}, bf16[16,64,1536]{2,1,0:T(8,128)(2,1)}, u32[]{:S(2)}, u32[]{:S(2)}) collective-permute-start(bf16[16,64,1536]{2,1,0:T(8,128)(2,1)} %bitcast.39), channel_id=1, source_target_pairs={{0,32},{32,64},{64,96},{96,0},{1,33},{33,65},{65,97},{97,1},{2,34}... | collective-permute-start | bytes 9437192 | tf_op jit(solution)/shard_map/ppermute | solution.py:23
  84.6 66.6 %collective-permute-start.1 = (bf16[16,64,1536]{2,1,0:T(8,128)(2,1)}, bf16[16,64,1536]{2,1,0:T(8,128)(2,1)}, u32[]{:S(2)}, u32[]{:S(2)}) collective-permute-start(bf16[16,64,1536]{2,1,0:T(8,128)(2,1)} %bitcast.40), channel_id=1, source_target_pairs={{0,96},{32,0},{64,32},{96,64},{1,97},{33,1},{65,33},{97,65},{2,98}... | collective-permute-start | bytes 9437192 | tf_op jit(solution)/shard_map/ppermute | solution.py:23
  88.8 69.7 %all-to-all-start = ((bf16[4,2,128,384]{3,2,1,0:T(8,128)(2,1)}), bf16[4,2,128,384]{3,2,1,0:T(8,128)(2,1)}, u32[]{:S(2)}, u32[]{:S(2)}) async-start(bf16[4,2,128,384]{3,2,1,0:T(8,128)(2,1)} %pad_maximum_fusion), calls=%async_computation | async-start | bytes 1572864 | tf_op jit(solution)/shard_map/all_to_all | solution.py:167
  147.7 8.1 %copy-start.5 = (s32[4]{0:T(128)S(1)}, s32[4]{0:T(128)}, u32[]{:S(2)}) copy-start(s32[4]{0:T(128)} %param.24) | copy-start | bytes 52
  147.7 30.2 %collective-permute-start.2 = (bf16[8,64,1536]{2,1,0:T(8,128)(2,1)}, bf16[8,64,1536]{2,1,0:T(8,128)(2,1)S(1)}, u32[]{:S(2)}, u32[]{:S(2)}) collective-permute-start(bf16[8,64,1536]{2,1,0:T(8,128)(2,1)} %slice.26), channel_id=1, source_target_pairs={{0,32},{32,64},{64,96},{96,0},{1,33},{33,65},{65,97},{97,1},{2,34}... | collective-permute-start | bytes 4718600 | tf_op jit(solution)/shard_map/ppermute | solution.py:23
  153.9 28.1 %collective-permute-start.3 = (bf16[8,64,1536]{2,1,0:T(8,128)(2,1)}, bf16[8,64,1536]{2,1,0:T(8,128)(2,1)}, u32[]{:S(2)}, u32[]{:S(2)}) collective-permute-start(bf16[8,64,1536]{2,1,0:T(8,128)(2,1)} %slice.27), channel_id=1, source_target_pairs={{0,96},{32,0},{64,32},{96,64},{1,97},{33,1},{65,33},{97,65},{2,98}... | collective-permute-start | bytes 4718600 | tf_op jit(solution)/shard_map/ppermute | solution.py:23
  182.9 1.6 collective-permute-start.4
  184.7 1.6 collective-permute-start.5
  190.3 1.6 collective-permute-start.6
  196.0 1.6 collective-permute-start.7
  201.5 1.6 collective-permute-start.8
  207.0 1.6 collective-permute-start.9
  212.5 128.9 %collective-permute-start.10 = (bf16[256,1536]{1,0:T(8,128)(2,1)}, bf16[256,1536]{1,0:T(8,128)(2,1)}, u32[]{:S(2)}, u32[]{:S(2)}) collective-permute-start(bf16[256,1536]{1,0:T(8,128)(2,1)} %get-tuple-element.269), channel_id=1, source_target_pairs={{24,28},{25,29},{26,30},{27,31},{56,60},{57,61},{58,62},{59,63},{8... | collective-permute-start | bytes 2359304 | tf_op jit(solution)/shard_map/ppermute | solution.py:180
Sparse Core Ops, SparseCore 0:
  10.7 71.7 all-gather.5
  84.5 93.0 all-gather.7
